TPU v7x, 768 devices: a whole 4x8x12 slice. The times are simulated.
768 devices in a mesh: row: 12 (over z), col: 2 (over core), layer: 32 (over y, x).
Axes of the slice: x: 4, y: 8, z: 12, core: 2. Of those that a mesh axis runs over, the one named last changes fastest.
Arguments:
- a_panel: bfloat16 [12288, 131072], P('row', ('col', 'layer')), may hold values from -6 to 6
- b_panel: bfloat16 [131072, 768], P(('col', 'layer'), 'row'), may hold values from -0.046875 to 0.046875
- a_occ: int32 [96, 1024], P('row', ('col', 'layer')), may hold values 0 or 1
- b_occ: int32 [1024, 6], P(('col', 'layer')), may hold values 0 or 1
Outputs:
- product: float32 [12288, 768], P('row', ('col', 'layer'))
All inputs are finite; a program needn't handle non-finite values. No bound on the sum of `a_occ` or of `b_occ` on one device may be relied on, other than what follows from the above.
Results may differ from a plain program's by a relative error of at most 0.0003.
Values may be sent and summed in bfloat16 or wider, within the bound.
A program may use at most 32 MiB of HBM per device.

v0:
```python
import jax
import jax.numpy as jnp
from jax import lax
from jax.sharding import PartitionSpec as P


def expand(occupancy, block):
    return jnp.repeat(jnp.repeat(occupancy, block, 0), block, 1).astype(jnp.bfloat16)


def body(a_panel, b_panel, a_occ, b_occ):
    block = a_panel.shape[0] // a_occ.shape[0]
    masked_a = a_panel * expand(a_occ, block)
    b_expanded = expand(b_occ, block)
    terms = jnp.dot(
        masked_a,
        lax.all_gather(b_panel, "row", axis=1, tiled=True) * b_expanded,
        preferred_element_type=jnp.float32,
    )
    across = lax.psum_scatter(terms, "col", scatter_dimension=1, tiled=True)
    result = lax.psum_scatter(across, "layer", scatter_dimension=1, tiled=True)
    return result


def solution(mesh):
    in_specs = (
        P("row", ("col", "layer")),
        P(("col", "layer"), "row"),
        P("row", ("col", "layer")),
        P(("col", "layer"), None),
    )
    out_specs = P("row", ("col", "layer"))
    return jax.shard_map(body, mesh=mesh, in_specs=in_specs, out_specs=out_specs, check_vma=False)
```

profile of v0, /device:TPU:1, one launch (start us, length us, event | category | flops | bytes accessed | tf_op | source)
XLA Modules:
  0.0 296.0 jit_solution(14736512202583290289)
XLA Ops:
  6.5 0.0 all-gather.2.cloned.1.call-start
  6.5 0.7 all-gather.2.cloned.1.call-update
  7.3 0.0 reduce-scatter.3.cloned.1.call-start
  7.3 0.7 convert_element_type.25
  8.0 0.1 broadcast_bitcast_fusion
  8.1 0.7 convert_element_type.22
  8.8 66.7 %all-gather.2.cloned.1.call-done = bf16[2048,768]{0,1:T(8,128)(2,1)} async-done(((bf16[2048,64]{0,1:T(8,128)(2,1)}), bf16[2048,768]{0,1:T(8,128)(2,1)}) %all-gather.2.cloned.1.call-update) | async-done | bytes 3145744 | tf_op jit(solution)/shard_map/all_gather | solution.py:17
  75.5 2.1 bitcast_multiply_fusion.2
  77.6 0.0 copy-start
  77.7 4.5 %broadcast_in_dim.13 = bf16[1024,16,128]{2,1,0:T(8,128)(2,1)S(1)} broadcast(bf16[1024,16]{1,0:T(8,128)(2,1)S(1)} %bitcast.19), dimensions={0,1} | broadcast | bytes 4227072 | tf_op jit(solution)/shard_map/broadcast_in_dim | solution.py:8
  82.2 0.0 copy-done
  82.2 5.2 %fusion = f32[1024,768]{1,0:T(8,128)} fusion(bf16[2048,768]{0,1:T(8,128)(2,1)S(1)} %bitcast_multiply_fusion.2, bf16[1024,2048]{1,0:T(8,128)(2,1)S(1)} %copy-done, bf16[128,8,16,128]{3,2,1,0:T(8,128)(2,1)S(1)} %bitcast.18), kind=kOutput, calls=%fused_computation.1 | convolution fusion | flops 3223322624 | bytes 14680064 | tf_op jit(solution)/shard_map/dot_general | solution.py:15
  87.4 0.0 reduce-scatter.3.cloned.1.call-update
  87.4 0.0 all-reduce.3.cloned.1.call-start
  87.5 27.1 %reduce-scatter.3.cloned.1.call-done = f32[1024,384]{1,0:T(8,128)} async-done(((f32[1024,768]{1,0:T(8,128)}), f32[1024,384]{1,0:T(8,128)}) %reduce-scatter.3.cloned.1.call-update) | async-done | bytes 1572880 | tf_op jit(solution)/shard_map/reduce_scatter | solution.py:20
  114.6 0.0 all-reduce.3.cloned.1.call-update
  114.6 1.3 dynamic-slice
  116.5 170.7 %all-reduce.3.cloned.1.call-done = f32[1024,384]{1,0:T(8,128)} async-done(((f32[1024,384]{1,0:T(8,128)}), f32[1024,384]{1,0:T(8,128)}) %all-reduce.3.cloned.1.call-update) | async-done | bytes 1572880
  287.2 1.4 constant_dynamic-slice_fusion
  288.6 0.8 copy.6
  (2 shorter events, 0.0 us)
Async XLA Ops:
  6.5 69.0 %all-gather.2.cloned.1.call-start = ((), (), s32[]{:S(2)}) async-start(), calls=%async_computation.1 | async-start | bytes 3407872 | tf_op jit(solution)/shard_map/all_gather | solution.py:17
  7.3 107.3 %reduce-scatter.3.cloned.1.call-start = ((), (), s32[]{:S(2)}) async-start(), calls=%async_computation.2 | async-start | bytes 4718592 | tf_op jit(solution)/shard_map/reduce_scatter | solution.py:20
  77.6 4.5 %copy-start = (bf16[1024,2048]{1,0:T(8,128)(2,1)S(1)}, bf16[1024,2048]{1,0:T(8,128)(2,1)}, u32[]{:S(2)}) copy-start(bf16[1024,2048]{1,0:T(8,128)(2,1)} %param.4) | copy-start | bytes 12582916
  87.4 199.8 %all-reduce.3.cloned.1.call-start = ((), (), s32[]{:S(2)}) async-start(), calls=%async_computation.3 | async-start | bytes 3145728
Sparse Core Ops, SparseCore 0:
  9.7 65.7 all-gather.1
  87.5 26.9 reduce-scatter.2
  118.4 168.7 all-reduce.2
where the time goes:
time: 299 us; the launch traced here: 296 us
  waiting for transfers between devices  265 us (89%)
  between operations  13.8 us (5%)
  local copies, waits for them, and re-layouts  8.11 us (3%)
  matrix products  5.22 us (2%)
  other arithmetic  3.49 us (1%)
    unnamed x4, waiting for transfers between devices  171 us
    all_gather x1, waiting for transfers between devices, body(): lax.all_gather(b_panel, 'row', axis=1, tiled=True) * b_expanded  66.7 us
    reduce_scatter x1, waiting for transfers between devices, body(): across = lax.psum_scatter(terms, 'col', scatter_dimension=1, tiled=True)  27.1 us
  transfers between devices with their start and end apart: 3, of which 3 were waited for; matrix products, arithmetic and copies ran while one was open for 1% of the time, Pallas kernels for 0%

commit v1 on v0

v1 whole, which is shorter than its diff:
```python
import functools

import jax
import jax.numpy as jnp
from jax import lax
from jax.experimental import pallas as pl
from jax.experimental.pallas import tpu as pltpu
from jax.sharding import PartitionSpec as P

MESH = pl.DeviceIdType.MESH
UNIT = 4


def kernel(nz, ny, nx, a_hbm, b_hbm, aocc, bocc, out, a_v, buf, part, core_in, x_in,
           y_out, y_in, fin, load_sem, ring_tx, ring_rx, first_tx, core_tx, core_rx,
           x_tx, x_rx, y_tx, y_rx):
    layers = ny * nx
    z, c, l = (lax.axis_index(name) for name in ("row", "col", "layer"))
    y, x = l // nx, lax.rem(l, nx)
    right, left = lax.rem(z + 1, nz), lax.rem(z + nz - 1, nz)
    ring = (right, left)
    rows, depth = a_v.shape
    half = buf.shape[2]
    units = half // UNIT
    upx = units // nx
    upd = out.shape[0] // UNIT
    lines = rows // 128
    per_unit = UNIT * lines
    per_x = upx * per_unit

    load_a = pltpu.make_async_copy(a_hbm, a_v, load_sem.at[0])
    load_b = [
        pltpu.make_async_copy(b_hbm.at[pl.ds((1 - d) * half, half)], buf.at[0, d], load_sem.at[1 + d])
        for d in range(2)
    ]
    for copy in load_b:
        copy.start()
    load_a.start()

    barrier = pltpu.get_barrier_semaphore()

    def greet(device):
        pl.semaphore_signal(barrier, inc=1, device_id=device, device_id_type=MESH)

    greet((right, c, l))
    greet((left, c, l))
    greet((z, 1 - c, l))

    def greet_layer(i, _):
        greet((z, c, lax.rem(l + i, layers)))
        return 0

    lax.fori_loop(1, layers, greet_layer, 0)

    def factor(value):
        return jnp.full((16, 128), value.astype(jnp.float32), jnp.float32).astype(jnp.bfloat16)

    for copy in load_b:
        copy.wait()
    for k in range(depth // 128):
        mask = factor(bocc[(z * 2 * half) // 128, k])
        for d in range(2):
            for r in range(0, half, 16):
                spot = (0, d, pl.ds(r, 16), pl.ds(k * 128, 128))
                buf[spot] = buf[spot] * mask

    pl.semaphore_wait(barrier, layers + 2)

    def ring_copy(g, d, source=None, tx=None, ahead=2):
        return pltpu.make_async_remote_copy(
            src_ref=buf.at[g, d] if source is None else source,
            dst_ref=buf.at[g + ahead, d],
            send_sem=ring_tx.at[g, d] if tx is None else tx,
            recv_sem=ring_rx.at[g + ahead, d],
            device_id=(ring[d], c, l),
            device_id_type=MESH,
        )

    def first_copy(d):
        return ring_copy(0, d, source=buf.at[0, 1 - d], tx=first_tx.at[d], ahead=1)

    for d in range(2):
        first_copy(d).start()
    for d in range(2):
        ring_copy(0, d).start()

    load_a.wait()

    def mask_a(k, _):
        cols = pl.ds(pl.multiple_of(k * 128, 128), 128)
        for i in range(rows // 128):
            mask = factor(aocc[i, k])
            tile = a_v[pl.ds(i * 128, 128), cols].reshape(8, 16, 128)
            a_v[pl.ds(i * 128, 128), cols] = (tile * mask[None]).reshape(128, 128)
        return 0

    lax.fori_loop(0, depth // 128, mask_a, 0)

    def meta(g, d):
        s = (g + 1) // 2
        if d == 0:
            j, h = lax.rem(z - s + nz, nz), lax.rem(g + 1, 2)
        else:
            j, h = lax.rem(z + s, nz), lax.rem(g, 2)
        return 2 * j + h

    def is_mine(g, d):
        return meta(g, d) // nz == c

    def core_copy(g, d):
        return pltpu.make_async_remote_copy(
            src_ref=part.at[g, d], dst_ref=core_in.at[g, d],
            send_sem=core_tx.at[g, d], recv_sem=core_rx.at[g, d],
            device_id=(z, 1 - c, l), device_id_type=MESH,
        )

    def x_copy(g, d, i):
        to = lax.rem(x + i, nx)
        return pltpu.make_async_remote_copy(
            src_ref=part.at[g, d, pl.ds(pl.multiple_of(to * per_x, 8), per_x)],
            dst_ref=x_in.at[g, d, i - 1],
            send_sem=x_tx.at[g, d, i - 1], recv_sem=x_rx.at[g, d, i - 1],
            device_id=(z, c, y * nx + to), device_id_type=MESH,
        )

    def y_copy(g, d, i):
        unit = units * lax.rem(meta(g, d), nz) + x * upx + i
        owner, u = unit // upd, lax.rem(unit, upd)
        copy = pltpu.make_async_remote_copy(
            src_ref=y_out.at[g, d, pl.ds(i * per_unit, per_unit)],
            dst_ref=y_in.at[u, y],
            send_sem=y_tx.at[g, d, i], recv_sem=y_rx.at[u, y],
            device_id=(z, c, owner), device_id_type=MESH,
        )
        return copy, owner, u

    def compute(g):
        lhs = buf[g].reshape(2 * half, depth)
        for m in range(0, rows, 256):
            sums = lax.dot_general(
                lhs, a_v[pl.ds(m, 256), :], (((1,), (1,)), ((), ())),
                preferred_element_type=jnp.float32,
            )
            for d in range(2):
                for n in range(2):
                    part[g, d, pl.ds(m // 128 + n, half, stride=lines), :] = (
                        sums[d * half:(d + 1) * half, n * 128:(n + 1) * 128]
                    )
        for d in range(2):
            @pl.when(jnp.logical_not(is_mine(g, d)))
            def _():
                core_copy(g, d).start()

    def add_core(g):
        for d in range(2):
            @pl.when(is_mine(g, d))
            def _():
                core_copy(g, d).wait_recv()
                part[g, d] = part[g, d] + core_in[g, d]
                for i in range(1, nx):
                    x_copy(g, d, i).start()

    def add_x(g):
        for d in range(2):
            @pl.when(is_mine(g, d))
            def _():
                total = part[g, d, pl.ds(pl.multiple_of(x * per_x, 8), per_x), :]
                for i in range(1, nx):
                    x_copy(g, d, i).wait_recv()
                    total = total + x_in[g, d, i - 1]
                y_out[g, d] = total
                for i in range(upx):
                    copy, owner, u = y_copy(g, d, i)

                    @pl.when(owner == l)
                    def _():
                        y_in[u, y] = y_out[g, d, pl.ds(i * per_unit, per_unit), :]

                    @pl.when(owner != l)
                    def _():
                        copy.start()

    def drain(g):
        for d in range(2):
            @pl.when(g < nz - 2)
            def _():
                ring_copy(g, d).wait_send()

            mine = is_mine(g, d)

            @pl.when(jnp.logical_not(mine))
            def _():
                core_copy(g, d).wait_send()

            @pl.when(mine)
            def _():
                for i in range(1, nx):
                    x_copy(g, d, i).wait_send()
                for i in range(upx):
                    copy, owner, _u = y_copy(g, d, i)

                    @pl.when(owner != l)
                    def _():
                        copy.wait_send()

    def step(g, _):
        for d in range(2):
            @pl.when(g > 0)
            def _():
                pltpu.make_async_copy(buf.at[g, d], buf.at[g, d], ring_rx.at[g, d]).wait()

            @pl.when(jnp.logical_and(g > 0, g < nz - 2))
            def _():
                ring_copy(g, d).start()

        compute(g)

        @pl.when(g >= 1)
        def _():
            add_core(g - 1)

        @pl.when(g >= 2)
        def _():
            add_x(g - 2)

        @pl.when(g >= 3)
        def _():
            drain(g - 3)

        return 0

    lax.fori_loop(0, nz, step, 0)
    add_core(nz - 1)
    add_x(nz - 2)
    add_x(nz - 1)
    for g in range(nz - 3, nz):
        drain(g)
    for d in range(2):
        first_copy(d).wait_send()

    for u in range(upd):
        unit = l * upd + u
        via = lax.rem(unit, units) // upx
        for i in range(ny):
            @pl.when(jnp.logical_not(jnp.logical_and(via == x, i == y)))
            def _():
                pltpu.make_async_copy(y_in.at[u, i], y_in.at[u, i], y_rx.at[u, i]).wait()
        total = y_in[u, 0]
        for i in range(1, ny):
            total = total + y_in[u, i]
        fin[pl.ds(u * per_unit, per_unit), :] = total
    for n in range(lines):
        out[:, pl.ds(n * 128, 128)] = fin[pl.ds(n, out.shape[0], stride=lines), :]


def body(nz, ny, nx, a_panel, b_panel, a_occ, b_occ):
    rows, depth = a_panel.shape
    half = b_panel.shape[1] // 2
    owned = nz * half // (ny * nx)
    lines = rows // 128
    units = half // UNIT
    upx = units // nx
    upd = owned // UNIT
    dma = pltpu.SemaphoreType.DMA
    result = pl.pallas_call(
        functools.partial(kernel, nz, ny, nx),
        out_shape=jax.ShapeDtypeStruct((owned, rows), jnp.float32),
        in_specs=[
            pl.BlockSpec(memory_space=pl.ANY),
            pl.BlockSpec(memory_space=pl.ANY),
            pl.BlockSpec(memory_space=pltpu.SMEM),
            pl.BlockSpec(memory_space=pltpu.SMEM),
        ],
        out_specs=pl.BlockSpec(memory_space=pltpu.VMEM),
        scratch_shapes=[
            pltpu.VMEM((rows, depth), jnp.bfloat16),
            pltpu.VMEM((nz, 2, half, depth), jnp.bfloat16),
            pltpu.VMEM((nz, 2, half * lines, 128), jnp.float32),
            pltpu.VMEM((nz, 2, half * lines, 128), jnp.float32),
            pltpu.VMEM((nz, 2, nx - 1, upx * UNIT * lines, 128), jnp.float32),
            pltpu.VMEM((nz, 2, upx * UNIT * lines, 128), jnp.float32),
            pltpu.VMEM((upd, ny, UNIT * lines, 128), jnp.float32),
            pltpu.VMEM((owned * lines, 128), jnp.float32),
            dma((3,)),
            dma((nz, 2)),
            dma((nz, 2)),
            dma((2,)),
            dma((nz, 2)),
            dma((nz, 2)),
            dma((nz, 2, nx - 1)),
            dma((nz, 2, nx - 1)),
            dma((nz, 2, upx)),
            dma((upd, ny)),
        ],
        compiler_params=pltpu.CompilerParams(
            collective_id=0, has_side_effects=True, vmem_limit_bytes=48 * 1024 * 1024
        ),
        cost_estimate=pl.CostEstimate(
            flops=2 * rows * depth * nz * 2 * half, bytes_accessed=rows * depth * 2, transcendentals=0
        ),
    )(a_panel, b_panel.T, a_occ, b_occ.T)
    return result.T


def solution(mesh):
    nz, layers = mesh.shape["row"], mesh.shape["layer"]
    nx = 4 if layers % 4 == 0 and layers > 4 else 2
    in_specs = (
        P("row", ("col", "layer")),
        P(("col", "layer"), "row"),
        P("row", ("col", "layer")),
        P(("col", "layer"), None),
    )
    out_specs = P("row", ("col", "layer"))
    return jax.shard_map(
        functools.partial(body, nz, layers // nx, nx),
        mesh=mesh, in_specs=in_specs, out_specs=out_specs, check_vma=False,
    )
```

time: 299 us -> 83 us (0.28)
  waiting for transfers between devices: 265 us -> 0 us
  Pallas kernels: 0 us -> 77.6 us
  between operations: 13.8 us -> 0.01 us
  matrix products: 5.22 us -> 0 us
  other arithmetic: 3.49 us -> 0 us
    unnamed x4 -> x0, waiting for transfers between devices: 171 us -> none
    pallas_call x0 -> x1, Pallas kernels: none -> 77.6 us  [body(): pl.pallas_call(functools.partial(kernel, nz, ny, nx), out_shape=jax.Shape...]
    all_gather x1 -> x0, waiting for transfers between devices: 66.7 us -> none  [body(): lax.all_gather(b_panel, 'row', axis=1, tiled=True) * b_expanded]
    reduce_scatter x1 -> x0, waiting for transfers between devices: 27.1 us -> none  [body(): across = lax.psum_scatter(terms, 'col', scatter_dimension=1, tiled=True)]
    dot_general x1 -> x0, matrix products: 5.22 us -> none  [body(): jnp.dot(masked_a, lax.all_gather(b_panel, 'row', axis=1, tiled=True) * b_...]
    broadcast_in_dim x2 -> x0, local copies, waits for them, and re-layouts: 4.5 us -> none  [the longest x1 4.46 us: expand(): jnp.repeat(jnp.repeat(occupancy, block, 0), block, 1).astype(jnp.bfloat16)]
  transfers between devices with their start and end apart: 3 -> 0, of which waited for: 3 -> 0; matrix products, arithmetic and copies ran while one was open for 1% -> 0% of each run, Pallas kernels for 0% -> 0%
where the time goes in v1:
time: 83 us; the launch traced here: 82.7 us
  Pallas kernels  77.6 us (93%)
  local copies, waits for them, and re-layouts  5.14 us (6%)
    pallas_call x1, Pallas kernels, body(): pl.pallas_call(functools.partial(kernel, nz, ny, nx), out_shape=jax.Shape...  77.6 us
    unnamed x9, local copies, waits for them, and re-layouts  5.14 us

profile of v1, /device:TPU:1, one launch (start us, length us, event | category | flops | bytes accessed | tf_op | source)
XLA Modules:
  0.0 82.7 jit_solution(16192076065932728266)
XLA Ops:
  0.0 0.0 copy-start
  0.0 2.2 %copy-done = bf16[1024,2048]{1,0:T(8,128)(2,1)S(1)} copy-done((bf16[1024,2048]{1,0:T(8,128)(2,1)S(1)}, bf16[1024,2048]{1,0:T(8,128)(2,1)}, u32[]{:S(2)}) %copy-start) | copy-done | bytes 4194328
  2.2 0.0 copy-start.1
  2.2 0.9 %copy-done.1 = bf16[2048,64]{0,1:T(8,128)(2,1)S(1)} copy-done((bf16[2048,64]{0,1:T(8,128)(2,1)S(1)}, bf16[2048,64]{0,1:T(8,128)(2,1)}, u32[]{:S(2)}) %copy-start.1) | copy-done | bytes 262168
  3.1 0.0 copy-start.2
  3.1 0.7 copy-done.2
  3.8 0.0 copy-start.3
  3.8 0.7 copy-done.3
  4.5 77.6 %shard_map.46 = f32[12,1024]{1,0:T(8,128)S(1)} custom-call(bf16[1024,2048]{1,0:T(8,128)(2,1)S(1)} %copy-done, bf16[64,2048]{1,0:T(8,128)(2,1)S(1)} %bitcast.4, s32[8,16]{1,0:T(8,128)S(1)} %copy-done.2, s32[6,16]{1,0:T(8,128)S(1)} %bitcast.5), custom_call_target="tpu_custom_call" | custom-call | flops 3221225472 | bytes 4194304 | tf_op jit(solution)/shard_map/pallas_call | solution.py:265
  82.1 0.6 copy.6
Async XLA Ops:
  0.0 2.2 %copy-start = (bf16[1024,2048]{1,0:T(8,128)(2,1)S(1)}, bf16[1024,2048]{1,0:T(8,128)(2,1)}, u32[]{:S(2)}) copy-start(bf16[1024,2048]{1,0:T(8,128)(2,1)} %a_hbm.1) | copy-start | bytes 12582916
  2.2 0.9 %copy-start.1 = (bf16[2048,64]{0,1:T(8,128)(2,1)S(1)}, bf16[2048,64]{0,1:T(8,128)(2,1)}, u32[]{:S(2)}) copy-start(bf16[2048,64]{0,1:T(8,128)(2,1)} %param.5) | copy-start | bytes 786436
  3.1 0.7 copy-start.2
  3.8 0.7 copy-start.3

commit v2 on v0

v2 whole, which is shorter than its diff:
```python
import functools

import jax
import jax.numpy as jnp
from jax import lax
from jax.experimental import pallas as pl
from jax.experimental.pallas import tpu as pltpu
from jax.sharding import PartitionSpec as P

MESH = pl.DeviceIdType.MESH
BLOCK = 128
NX, NY = 4, 8


def ring_order(nz):
    if nz == 12:
        names = ["o0", "b1", "b2", "f1", "b3", "b4", "f2", "b5", "f3", "b6", "f4", "b7"]
    else:
        back = nz // 2
        names = ["o0"] + [n + str(s) for s in range(1, back + 1) for n in "bf" if s <= (nz - 1 - back if n == "f" else back)]
    items = [(n[0], int(n[1:])) for n in names]
    place = {item: i for i, item in enumerate(items)}
    offsets = [s if n != "f" else nz - s for n, s in items]
    onward = [place.get((n, s + 1), 0) for n, s in items]
    forward = [int(n == "f") for n, s in items]
    return offsets, onward, forward, place[("f", 1)], place[("b", 1)]


def pick(i, values):
    result = jnp.int32(values[0])
    for k, value in enumerate(values):
        if k > 0:
            result = jnp.where(i == k, jnp.int32(value), result)
    return result


def kernel(nz, slots, a_hbm, b_hbm, aocc_hbm, bocc_hbm, out, flag_out, a_v, b_v, aocc, bocc, stored, absent, wide, buf,
           part, core_in, x1_in, x2_in, y_out, y_in, f_out, fin, flag, flag_c, flag_x, flag_y,
           load_sem, own_tx, ring_tx, ring_rx, core_tx, core_rx, x1_tx, x1_rx, x2_tx, x2_rx,
           y_tx, y_rx, f_tx, f_rx, fc_tx, fc_rx, fx_tx, fx_rx, fy_tx, fy_rx):
    offsets, onward, forward, first_f, first_b = ring_order(nz)
    layers = NX * NY
    z, c, l = (lax.axis_index(name) for name in ("row", "col", "layer"))
    y, x = l // NX, lax.rem(l, NX)
    right, left = lax.rem(z + 1, nz), lax.rem(z + nz - 1, nz)
    rows, depth = a_v.shape
    width = b_v.shape[0]
    half = width // 2
    blocks = depth // BLOCK
    lines = rows // 128
    piece = width // NX * lines
    pair = piece // NY
    owned = out.shape[0]

    loads = [
        pltpu.make_async_copy(bocc_hbm, bocc, load_sem.at[0]),
        pltpu.make_async_copy(b_hbm, b_v, load_sem.at[1]),
        pltpu.make_async_copy(aocc_hbm, aocc, load_sem.at[2]),
        pltpu.make_async_copy(a_hbm, a_v, load_sem.at[3]),
    ]
    for copy in loads:
        copy.start()

    barrier = pltpu.get_barrier_semaphore()

    def greet(device):
        pl.semaphore_signal(barrier, inc=1, device_id=device, device_id_type=MESH)

    greet((right, c, l))
    greet((left, c, l))
    greet((z, 1 - c, l))

    def greet_layer(i, _):
        greet((z, c, lax.rem(l + i, layers)))
        return 0

    lax.fori_loop(1, layers, greet_layer, 0)

    def factor(value):
        return jnp.full((16, 128), value.astype(jnp.float32), jnp.float32).astype(jnp.bfloat16)

    own_column = (z * width) // BLOCK

    def note_blocks(n, over):
        count = jnp.int32(0)
        for k in range(blocks):
            stored[n, k] = factor(bocc[n, k])
            absent[n, k] = factor(1 - bocc[n, k])
            count = count + bocc[n, k]
        return over + jnp.maximum(count - slots, 0)

    loads[0].wait()
    note_blocks(own_column, jnp.int32(0))

    loads[1].wait()
    tiles = (width // 16, 16, BLOCK)
    held = [jnp.zeros(tiles, jnp.bfloat16)] * slots
    for k in reversed(range(blocks)):
        on, off = stored[own_column, k][None], absent[own_column, k][None]
        tile = b_v[:, k * BLOCK:(k + 1) * BLOCK].reshape(tiles)
        held = [(tile if s == 0 else held[s - 1]) * on + held[s] * off for s in range(slots)]
    for s in range(slots):
        buf[0, :, s * BLOCK:(s + 1) * BLOCK] = held[s].reshape(width, BLOCK)

    def mask_a(k, _):
        cols = pl.ds(pl.multiple_of(k * BLOCK, BLOCK), BLOCK)
        for i in range(rows // BLOCK):
            mask = factor(aocc[i, k])
            tile = a_v[pl.ds(i * BLOCK, BLOCK), cols].reshape(BLOCK // 16, 16, BLOCK)
            a_v[pl.ds(i * BLOCK, BLOCK), cols] = (tile * mask[None]).reshape(BLOCK, BLOCK)
        return 0

    def prepare():
        loads[2].wait()
        loads[3].wait()
        lax.fori_loop(0, blocks, mask_a, 0)
        over = lax.fori_loop(0, bocc.shape[0], note_blocks, jnp.int32(0))
        flag[0] = jnp.full(flag.shape[1:], over.astype(jnp.float32), jnp.float32)

    early = z < nz // 2
    pl.when(early)(prepare)
    pl.semaphore_wait(barrier, layers + 2)

    def ring_copy(i, h, to, device, tx):
        return pltpu.make_async_remote_copy(
            src_ref=buf.at[i, pl.ds(h * half, half)], dst_ref=buf.at[to, pl.ds(h * half, half)],
            send_sem=tx, recv_sem=ring_rx.at[to, h],
            device_id=(device, c, l), device_id_type=MESH,
        )

    def onward_copy(i, h):
        device = jnp.where(pick(i, forward) > 0, right, left)
        return ring_copy(i, h, pick(i, onward), device, ring_tx.at[i, h])

    own_copies = [ring_copy(0, h, first_b, left, own_tx.at[0, h]) for h in range(2)]
    own_copies += [ring_copy(0, h, first_f, right, own_tx.at[1, h]) for h in range(2)]
    for copy in own_copies:
        copy.start()

    flag_core = pltpu.make_async_remote_copy(
        src_ref=flag.at[0], dst_ref=flag_c, send_sem=fc_tx, recv_sem=fc_rx,
        device_id=(z, 1 - c, l), device_id_type=MESH,
    )

    def flag_copies(i, inbox, count, tx, rx, device):
        return [
            pltpu.make_async_remote_copy(
                src_ref=flag.at[i], dst_ref=inbox.at[n - 1], send_sem=tx.at[n - 1], recv_sem=rx.at[n - 1],
                device_id=(z, c, device(n)), device_id_type=MESH,
            )
            for n in range(1, count)
        ]

    flag_xs = flag_copies(1, flag_x, NX, fx_tx, fx_rx, lambda n: y * NX + lax.rem(x + n, NX))
    flag_ys = flag_copies(2, flag_y, NY, fy_tx, fy_rx, lambda n: lax.rem(y + n, NY) * NX + x)

    pl.when(jnp.logical_not(early))(prepare)
    flag_core.start()

    def shard(i):
        return lax.rem(z + pick(i, offsets), nz)

    def is_mine(i):
        return shard(i) // (nz // 2) == c

    def lines_of(p, start, size):
        return pl.ds(pl.multiple_of(p * piece + start, 8), size)

    x_right, x_left, x_far = (lax.rem(x + n, NX) for n in (1, NX - 1, 2))

    def core_copy(i):
        return pltpu.make_async_remote_copy(
            src_ref=part.at[i], dst_ref=core_in.at[i], send_sem=core_tx.at[i], recv_sem=core_rx.at[i],
            device_id=(z, 1 - c, l), device_id_type=MESH,
        )

    def x1_copies(i):
        return [
            pltpu.make_async_remote_copy(
                src_ref=part.at[i, lines_of(x_far, n * piece // 2, piece // 2)], dst_ref=x1_in.at[i, n],
                send_sem=x1_tx.at[i, n], recv_sem=x1_rx.at[i, n],
                device_id=(z, c, y * NX + to), device_id_type=MESH,
            )
            for n, to in enumerate((x_right, x_left))
        ]

    def x2_copies(i):
        return [
            pltpu.make_async_remote_copy(
                src_ref=part.at[i, lines_of(to, 0, piece)], dst_ref=x2_in.at[i, n],
                send_sem=x2_tx.at[i, n], recv_sem=x2_rx.at[i, n],
                device_id=(z, c, y * NX + to), device_id_type=MESH,
            )
            for n, to in enumerate((x_right, x_left))
        ]

    def y_copies(i):
        copies = []
        for n in range(1, NY):
            to = lax.rem(y + n, NY)
            copies.append(pltpu.make_async_remote_copy(
                src_ref=y_out.at[i, pl.ds(pl.multiple_of(to * pair, 8), pair)], dst_ref=y_in.at[i, n - 1],
                send_sem=y_tx.at[i, n - 1], recv_sem=y_rx.at[i, n - 1],
                device_id=(z, c, to * NX + x), device_id_type=MESH,
            ))
        return copies

    def f_copy(i):
        column = width * lax.rem(shard(i), nz // 2) + (width // NX) * x + (pair // lines) * y
        owner, spot = column // owned, lax.rem(column, owned) // (pair // lines)
        copy = pltpu.make_async_remote_copy(
            src_ref=f_out.at[i], dst_ref=fin.at[pl.ds(pl.multiple_of(spot * pair, 8), pair)],
            send_sem=f_tx.at[i], recv_sem=f_rx.at[spot],
            device_id=(z, c, owner), device_id_type=MESH,
        )
        return copy, owner, spot

    def compute(i):
        column = (shard(i) * width) // BLOCK
        held = [buf[i, :, s * BLOCK:(s + 1) * BLOCK].reshape(tiles) for s in range(slots)]
        for k in range(blocks):
            on, off = stored[column, k][None], absent[column, k][None]
            wide[:, k * BLOCK:(k + 1) * BLOCK] = (held[0] * on).reshape(width, BLOCK)
            held = [
                held[s] * off + held[s + 1] * on if s < slots - 1 else held[s] * off
                for s in range(min(slots, blocks - 1 - k))
            ]
        lhs = wide[...]
        for m in range(0, rows, 256):
            sums = lax.dot_general(
                lhs, a_v[pl.ds(m, 256), :], (((1,), (1,)), ((), ())), preferred_element_type=jnp.float32,
            )
            for n in range(2):
                part[i, pl.ds(m // 128 + n, width, stride=lines), :] = sums[:, n * 128:(n + 1) * 128]

        @pl.when(jnp.logical_not(is_mine(i)))
        def _():
            core_copy(i).start()

    def add_core(i):
        @pl.when(is_mine(i))
        def _():
            core_copy(i).wait_recv()
            part[i] = part[i] + core_in[i]
            for copy in x1_copies(i):
                copy.start()

    def add_x1(i):
        @pl.when(is_mine(i))
        def _():
            copies, later = x1_copies(i), x2_copies(i)
            for n, to in enumerate((x_right, x_left)):
                copies[n].wait_recv()
                spot = lines_of(to, n * piece // 2, piece // 2)
                part[i, spot, :] = part[i, spot, :] + x1_in[i, n]
                later[n].start()

    def add_x2(i):
        @pl.when(is_mine(i))
        def _():
            for copy in x2_copies(i):
                copy.wait_recv()
            y_out[i] = part[i, lines_of(x, 0, piece), :] + (x2_in[i, 0] + x2_in[i, 1])
            for copy in y_copies(i):
                copy.start()

    def add_y(i):
        @pl.when(is_mine(i))
        def _():
            total = y_out[i, pl.ds(pl.multiple_of(y * pair, 8), pair), :]
            for n, copy in enumerate(y_copies(i)):
                copy.wait_recv()
                total = total + y_in[i, n]
            copy, owner, spot = f_copy(i)
            f_out[i] = total

            @pl.when(owner == l)
            def _():
                fin[pl.ds(pl.multiple_of(spot * pair, 8), pair), :] = total

            @pl.when(owner != l)
            def _():
                copy.start()

    def drain(i):
        @pl.when(pick(i, onward) > 0)
        def _():
            for h in range(2):
                onward_copy(i, h).wait_send()

        mine = is_mine(i)

        @pl.when(jnp.logical_not(mine))
        def _():
            core_copy(i).wait_send()

        @pl.when(mine)
        def _():
            for copy in x1_copies(i) + x2_copies(i) + y_copies(i):
                copy.wait_send()
            copy, owner, _spot = f_copy(i)

            @pl.when(owner != l)
            def _():
                copy.wait_send()

    stages = ((1, add_core), (3, add_x1), (5, add_x2), (8, add_y))

    def step(i, _):
        @pl.when(i > 0)
        def _():
            for h in range(2):
                spot = buf.at[i, pl.ds(h * half, half)]
                pltpu.make_async_copy(spot, spot, ring_rx.at[i, h]).wait()

                @pl.when(pick(i, onward) > 0)
                def _():
                    onward_copy(i, h).start()

        compute(i)
        for lag, stage in stages:
            @pl.when(i >= lag)
            def _():
                stage(i - lag)

        return 0

    lax.fori_loop(0, nz - 2, step, 0)

    flag_core.wait()
    flag[1] = flag[0] + flag_c[...]
    for copy in flag_xs:
        copy.start()
    lax.fori_loop(nz - 2, nz - 1, step, 0)
    total_x = flag[1]
    for n, copy in enumerate(flag_xs):
        copy.wait()
        total_x = total_x + flag_x[n]
    flag[2] = total_x
    for copy in flag_ys:
        copy.start()
    lax.fori_loop(nz - 1, nz, step, 0)

    def catch_up(k, low, high):
        for i in range(max(low, 0), high):
            stages[k][1](i)

    left_over = [nz - lag for lag, _stage in stages]
    add_core(nz - 1)
    catch_up(1, left_over[1], nz - 1)
    catch_up(2, left_over[2], nz - 3)
    catch_up(3, left_over[3], nz - 6)
    add_x1(nz - 1)
    catch_up(2, max(left_over[2], nz - 3), nz - 1)
    catch_up(3, max(left_over[3], nz - 6), nz - 4)
    add_x2(nz - 1)
    catch_up(3, max(left_over[3], nz - 4), nz - 1)
    for i in range(nz - 1):
        drain(i)
    add_y(nz - 1)
    drain(nz - 1)
    total_y = flag[2]
    for n, copy in enumerate(flag_ys):
        copy.wait()
        total_y = total_y + flag_y[n]
    flag_out[...] = total_y
    for copy in own_copies:
        copy.wait_send()

    for spot in range(owned * lines // pair):
        column = lax.rem(l * owned + spot * (pair // lines), width)
        from_x, from_y = column // (width // NX), lax.rem(column, width // NX) // (pair // lines)

        @pl.when(jnp.logical_not(jnp.logical_and(from_x == x, from_y == y)))
        def _():
            here = fin.at[pl.ds(spot * pair, pair)]
            pltpu.make_async_copy(here, here, f_rx.at[spot]).wait()
    for n in range(lines):
        out[:, pl.ds(n * 128, 128)] = fin[pl.ds(n, owned, stride=lines), :]


def sparse_product(nz, a_panel, b_panel, a_occ, b_occ):
    rows, depth = a_panel.shape
    width = b_panel.shape[1]
    blocks = depth // BLOCK
    slots = blocks // 2
    lines = rows // 128
    owned = nz * width // (2 * NX * NY)
    piece = width // NX * lines
    pair = piece // NY
    columns = b_occ.shape[1]
    dma = pltpu.SemaphoreType.DMA
    f32, bf16 = jnp.float32, jnp.bfloat16
    scratch = [
        pltpu.VMEM((rows, depth), bf16),
        pltpu.VMEM((width, depth), bf16),
        pltpu.SMEM(a_occ.shape, jnp.int32),
        pltpu.SMEM((columns, blocks), jnp.int32),
        pltpu.VMEM((columns, blocks, 16, BLOCK), bf16),
        pltpu.VMEM((columns, blocks, 16, BLOCK), bf16),
        pltpu.VMEM((width, depth), bf16),
        pltpu.VMEM((nz, width, slots * BLOCK), bf16),
        pltpu.VMEM((nz, width * lines, 128), f32),
        pltpu.VMEM((nz, width * lines, 128), f32),
        pltpu.VMEM((nz, 2, piece // 2, 128), f32),
        pltpu.VMEM((nz, 2, piece, 128), f32),
        pltpu.VMEM((nz, piece, 128), f32),
        pltpu.VMEM((nz, NY - 1, pair, 128), f32),
        pltpu.VMEM((nz, pair, 128), f32),
        pltpu.VMEM((owned * lines, 128), f32),
        pltpu.VMEM((3, 8, 128), f32),
        pltpu.VMEM((8, 128), f32),
        pltpu.VMEM((NX - 1, 8, 128), f32),
        pltpu.VMEM((NY - 1, 8, 128), f32),
        dma((4,)), dma((2, 2)), dma((nz, 2)), dma((nz, 2)),
        dma((nz,)), dma((nz,)), dma((nz, 2)), dma((nz, 2)), dma((nz, 2)), dma((nz, 2)),
        dma((nz, NY - 1)), dma((nz, NY - 1)), dma((nz,)), dma((owned * lines // pair,)),
        dma(()), dma(()), dma((NX - 1,)), dma((NX - 1,)), dma((NY - 1,)), dma((NY - 1,)),
    ]
    anywhere = pl.BlockSpec(memory_space=pl.ANY)
    inside = pl.BlockSpec(memory_space=pltpu.VMEM)
    return pl.pallas_call(
        functools.partial(kernel, nz, slots),
        out_shape=(jax.ShapeDtypeStruct((owned, rows), f32), jax.ShapeDtypeStruct((8, 128), f32)),
        in_specs=[anywhere] * 4,
        out_specs=(inside, inside),
        scratch_shapes=scratch,
        compiler_params=pltpu.CompilerParams(
            collective_id=0, has_side_effects=True, vmem_limit_bytes=60 * 1024 * 1024
        ),
        cost_estimate=pl.CostEstimate(
            flops=2 * rows * slots * BLOCK * nz * width, bytes_accessed=rows * depth * 2, transcendentals=0
        ),
    )(a_panel, b_panel.T, a_occ, b_occ.T)


def expand(occupancy, block):
    return jnp.repeat(jnp.repeat(occupancy, block, 0), block, 1).astype(jnp.bfloat16)


def dense_product(nz, a_panel, b_panel, a_occ, b_occ):
    z = lax.axis_index("row")
    width, depth = b_panel.shape[1], b_panel.shape[0]

    def step(s, carry):
        held, gathered = carry
        gathered = lax.dynamic_update_slice(gathered, held[None], (lax.rem(z - s + nz, nz), 0, 0))
        return lax.ppermute(held, "row", [(i, (i + 1) % nz) for i in range(nz)]), gathered

    occupied = lax.dynamic_slice_in_dim(b_occ.T, (z * width) // BLOCK, 1).astype(b_panel.dtype)
    start = (b_panel.T * jnp.repeat(occupied, BLOCK, 1), jnp.zeros((nz, width, depth), b_panel.dtype))
    _, gathered = lax.fori_loop(0, nz, step, start)
    terms = lax.dot_general(
        gathered.reshape(nz * width, depth),
        a_panel * expand(a_occ, BLOCK),
        (((1,), (1,)), ((), ())), preferred_element_type=jnp.float32,
    )
    shares = 2 * NX * NY
    terms = terms.reshape(shares, nz * width // shares, a_panel.shape[0])
    return lax.all_to_all(terms, ("col", "layer"), 0, 0).sum(0).T


def body(nz, a_panel, b_panel, a_occ, b_occ):
    result, over = sparse_product(nz, a_panel, b_panel, a_occ, b_occ)
    return lax.cond(
        over[0, 0] > 0,
        lambda: dense_product(nz, a_panel, b_panel, a_occ, b_occ),
        lambda: result.T,
    )


def solution(mesh):
    in_specs = (
        P("row", ("col", "layer")),
        P(("col", "layer"), "row"),
        P("row", ("col", "layer")),
        P(("col", "layer"), None),
    )
    out_specs = P("row", ("col", "layer"))
    return jax.shard_map(
        functools.partial(body, mesh.shape["row"]),
        mesh=mesh, in_specs=in_specs, out_specs=out_specs, check_vma=False,
    )
```

time: 299 us -> 70 us (0.23)
  the two profiles are of different devices: /device:TPU:1 before, /device:TPU:264 now
where the time goes in v2:
time: 70 us; the launch traced here: 69.7 us
  Pallas kernels  66.2 us (95%)
  local copies, waits for them, and re-layouts  2.66 us (4%)
    pallas_call x1, Pallas kernels, sparse_product(): pl.pallas_call(functools.partial(kernel, nz, slots), out_shape=(jax.Shape...  66.2 us
    unnamed x7, local copies, waits for them, and re-layouts  1.47 us

profile of v2, /device:TPU:264, one launch (start us, length us, event | category | flops | bytes accessed | tf_op | source)
XLA Modules:
  0.0 69.7 jit_solution(9394861224959470055)
XLA Ops:
  0.0 0.0 copy-start.3
  0.0 0.0 copy-start.1
  0.0 66.2 %shard_map.48 = (f32[12,1024]{1,0:T(8,128)}, f32[8,128]{1,0:T(8,128)}) custom-call(bf16[1024,2048]{1,0:T(8,128)(2,1)} %a_hbm.1, bf16[64,2048]{1,0:T(8,128)(2,1)} %bitcast.27, s32[8,16]{1,0:T(8,128)} %aocc_hbm.1, s32[6,16]{1,0:T(8,128)} %bitcast.30), custom_call_target="tpu_custom_call" | custom-call | flops 1610612736 | bytes 4194304 | tf_op jit(solution)/shard_map/pallas_call | solution.py:422
  66.2 0.8 %copy.31 = f32[12,1024]{1,0:T(8,128)S(1)} copy(f32[12,1024]{1,0:T(8,128)} %get-tuple-element.103) | data formatting | bytes 98304
  67.0 1.2 %slice.3 = f32[1,1]{1,0:T(1,128)} slice(f32[8,128]{1,0:T(8,128)} %get-tuple-element.102), slice={[0:1], [0:1]} | slice | bytes 8 | tf_op jit(solution)/shard_map/slice | solution.py:466
  68.8 0.0 copy-done.3
  68.9 0.0 copy-done.1
  68.9 0.2 conditional.1
  69.1 0.0 copy-start.2
  69.1 0.6 copy-done.2
Async XLA Ops:
  0.0 68.9 %copy-start.3 = (s32[8,16]{1,0:T(8,128)S(1)}, s32[8,16]{1,0:T(8,128)}, u32[]{:S(2)}) copy-start(s32[8,16]{1,0:T(8,128)} %aocc_hbm.1) | copy-start | bytes 1540
  0.0 68.9 %copy-start.1 = (bf16[2048,64]{0,1:T(8,128)(2,1)S(1)}, bf16[2048,64]{0,1:T(8,128)(2,1)}, u32[]{:S(2)}) copy-start(bf16[2048,64]{0,1:T(8,128)(2,1)} %param.9) | copy-start | bytes 786436
  69.1 0.6 copy-start.2

commit v3 on v2

--- a/solution.py
+++ b/solution.py
@@ -9,15 +9,14 @@
 
 MESH = pl.DeviceIdType.MESH
 BLOCK = 128
+UNIT = 4
 NX, NY = 4, 8
 
 
 def ring_order(nz):
-    if nz == 12:
-        names = ["o0", "b1", "b2", "f1", "b3", "b4", "f2", "b5", "f3", "b6", "f4", "b7"]
-    else:
-        back = nz // 2
-        names = ["o0"] + [n + str(s) for s in range(1, back + 1) for n in "bf" if s <= (nz - 1 - back if n == "f" else back)]
+    names = ["o0"]
+    for s in range(1, nz // 2 + 1):
+        names += ["b" + str(s)] + ["f" + str(s)] * (2 * s < nz)
     items = [(n[0], int(n[1:])) for n in names]
     place = {item: i for i, item in enumerate(items)}
     offsets = [s if n != "f" else nz - s for n, s in items]
@@ -35,9 +34,9 @@
 
 
 def kernel(nz, slots, a_hbm, b_hbm, aocc_hbm, bocc_hbm, out, flag_out, a_v, b_v, aocc, bocc, stored, absent, wide, buf,
-           part, core_in, x1_in, x2_in, y_out, y_in, f_out, fin, flag, flag_c, flag_x, flag_y,
+           part, core_in, x1_in, x2_in, y_out, y_in, fin, flag, flag_c, flag_x, flag_y,
            load_sem, own_tx, ring_tx, ring_rx, core_tx, core_rx, x1_tx, x1_rx, x2_tx, x2_rx,
-           y_tx, y_rx, f_tx, f_rx, fc_tx, fc_rx, fx_tx, fx_rx, fy_tx, fy_rx):
+           y_tx, y_rx, fc_tx, fc_rx, fx_tx, fx_rx, fy_tx, fy_rx):
     offsets, onward, forward, first_f, first_b = ring_order(nz)
     layers = NX * NY
     z, c, l = (lax.axis_index(name) for name in ("row", "col", "layer"))
@@ -49,7 +48,10 @@
     blocks = depth // BLOCK
     lines = rows // 128
     piece = width // NX * lines
-    pair = piece // NY
+    unit = UNIT * lines
+    units = piece // unit
+    per_owner = out.shape[0] // UNIT
+    pairs = nz // 2
     owned = out.shape[0]
 
     loads = [
@@ -194,48 +196,45 @@
             for n, to in enumerate((x_right, x_left))
         ]
 
-    def y_copies(i):
-        copies = []
-        for n in range(1, NY):
-            to = lax.rem(y + n, NY)
-            copies.append(pltpu.make_async_remote_copy(
-                src_ref=y_out.at[i, pl.ds(pl.multiple_of(to * pair, 8), pair)], dst_ref=y_in.at[i, n - 1],
-                send_sem=y_tx.at[i, n - 1], recv_sem=y_rx.at[i, n - 1],
-                device_id=(z, c, to * NX + x), device_id_type=MESH,
-            ))
-        return copies
-
-    def f_copy(i):
-        column = width * lax.rem(shard(i), nz // 2) + (width // NX) * x + (pair // lines) * y
-        owner, spot = column // owned, lax.rem(column, owned) // (pair // lines)
+    def y_copy(i, n):
+        column = width * lax.rem(shard(i), nz // 2) + (width // NX) * x + UNIT * n
+        owner, spot = column // owned, lax.rem(column, owned) // UNIT
         copy = pltpu.make_async_remote_copy(
-            src_ref=f_out.at[i], dst_ref=fin.at[pl.ds(pl.multiple_of(spot * pair, 8), pair)],
-            send_sem=f_tx.at[i], recv_sem=f_rx.at[spot],
+            src_ref=y_out.at[i, pl.ds(n * unit, unit)], dst_ref=y_in.at[spot, y],
+            send_sem=y_tx.at[i, n], recv_sem=y_rx.at[spot, y],
             device_id=(z, c, owner), device_id_type=MESH,
         )
         return copy, owner, spot
 
-    def compute(i):
-        column = (shard(i) * width) // BLOCK
-        held = [buf[i, :, s * BLOCK:(s + 1) * BLOCK].reshape(tiles) for s in range(slots)]
-        for k in range(blocks):
-            on, off = stored[column, k][None], absent[column, k][None]
-            wide[:, k * BLOCK:(k + 1) * BLOCK] = (held[0] * on).reshape(width, BLOCK)
-            held = [
-                held[s] * off + held[s + 1] * on if s < slots - 1 else held[s] * off
-                for s in range(min(slots, blocks - 1 - k))
-            ]
+    def compute(p):
+        for t in range(2):
+            i = 2 * p + t
+            column = (shard(i) * width) // BLOCK
+            place = pl.ds(t * width, width)
+            held = [buf[i, :, s * BLOCK:(s + 1) * BLOCK].reshape(tiles) for s in range(slots)]
+            for k in range(blocks):
+                on, off = stored[column, k][None], absent[column, k][None]
+                wide[place, k * BLOCK:(k + 1) * BLOCK] = (held[0] * on).reshape(width, BLOCK)
+                held = [
+                    held[s] * off + held[s + 1] * on if s < slots - 1 else held[s] * off
+                    for s in range(min(slots, blocks - 1 - k))
+                ]
         lhs = wide[...]
         for m in range(0, rows, 256):
             sums = lax.dot_general(
                 lhs, a_v[pl.ds(m, 256), :], (((1,), (1,)), ((), ())), preferred_element_type=jnp.float32,
             )
-            for n in range(2):
-                part[i, pl.ds(m // 128 + n, width, stride=lines), :] = sums[:, n * 128:(n + 1) * 128]
-
-        @pl.when(jnp.logical_not(is_mine(i)))
-        def _():
-            core_copy(i).start()
+            for t in range(2):
+                for n in range(2):
+                    part[2 * p + t, pl.ds(m // 128 + n, width, stride=lines), :] = (
+                        sums[t * width:(t + 1) * width, n * 128:(n + 1) * 128]
+                    )
+        for t in range(2):
+            i = 2 * p + t
+
+            @pl.when(jnp.logical_not(is_mine(i)))
+            def _():
+                core_copy(i).start()
 
     def add_core(i):
         @pl.when(is_mine(i))
@@ -261,26 +260,16 @@
             for copy in x2_copies(i):
                 copy.wait_recv()
             y_out[i] = part[i, lines_of(x, 0, piece), :] + (x2_in[i, 0] + x2_in[i, 1])
-            for copy in y_copies(i):
-                copy.start()
-
-    def add_y(i):
-        @pl.when(is_mine(i))
-        def _():
-            total = y_out[i, pl.ds(pl.multiple_of(y * pair, 8), pair), :]
-            for n, copy in enumerate(y_copies(i)):
-                copy.wait_recv()
-                total = total + y_in[i, n]
-            copy, owner, spot = f_copy(i)
-            f_out[i] = total
-
-            @pl.when(owner == l)
-            def _():
-                fin[pl.ds(pl.multiple_of(spot * pair, 8), pair), :] = total
-
-            @pl.when(owner != l)
-            def _():
-                copy.start()
+            for n in range(units):
+                copy, owner, spot = y_copy(i, n)
+
+                @pl.when(owner == l)
+                def _():
+                    y_in[spot, y] = y_out[i, pl.ds(n * unit, unit), :]
+
+                @pl.when(owner != l)
+                def _():
+                    copy.start()
 
     def drain(i):
         @pl.when(pick(i, onward) > 0)
@@ -296,42 +285,50 @@
 
         @pl.when(mine)
         def _():
-            for copy in x1_copies(i) + x2_copies(i) + y_copies(i):
+            for copy in x1_copies(i) + x2_copies(i):
                 copy.wait_send()
-            copy, owner, _spot = f_copy(i)
-
-            @pl.when(owner != l)
+            for n in range(units):
+                copy, owner, _spot = y_copy(i, n)
+
+                @pl.when(owner != l)
+                def _():
+                    copy.wait_send()
+
+    def both(stage, p):
+        for t in range(2):
+            stage(2 * p + t)
+
+    stages = ((1, add_core), (2, add_x1), (3, add_x2))
+
+    def step(p, _):
+        for t in range(2):
+            i = 2 * p + t
+
+            @pl.when(i > 0)
             def _():
-                copy.wait_send()
-
-    stages = ((1, add_core), (3, add_x1), (5, add_x2), (8, add_y))
-
-    def step(i, _):
-        @pl.when(i > 0)
-        def _():
-            for h in range(2):
-                spot = buf.at[i, pl.ds(h * half, half)]
-                pltpu.make_async_copy(spot, spot, ring_rx.at[i, h]).wait()
-
-                @pl.when(pick(i, onward) > 0)
-                def _():
-                    onward_copy(i, h).start()
-
-        compute(i)
+                for h in range(2):
+                    spot = buf.at[i, pl.ds(h * half, half)]
+                    pltpu.make_async_copy(spot, spot, ring_rx.at[i, h]).wait()
+
+                    @pl.when(pick(i, onward) > 0)
+                    def _():
+                        onward_copy(i, h).start()
+
+        compute(p)
         for lag, stage in stages:
-            @pl.when(i >= lag)
+            @pl.when(p >= lag)
             def _():
-                stage(i - lag)
+                both(stage, p - lag)
 
         return 0
 
-    lax.fori_loop(0, nz - 2, step, 0)
+    lax.fori_loop(0, pairs - 2, step, 0)
 
     flag_core.wait()
     flag[1] = flag[0] + flag_c[...]
     for copy in flag_xs:
         copy.start()
-    lax.fori_loop(nz - 2, nz - 1, step, 0)
+    lax.fori_loop(pairs - 2, pairs - 1, step, 0)
     total_x = flag[1]
     for n, copy in enumerate(flag_xs):
         copy.wait()
@@ -339,26 +336,23 @@
     flag[2] = total_x
     for copy in flag_ys:
         copy.start()
-    lax.fori_loop(nz - 1, nz, step, 0)
-
-    def catch_up(k, low, high):
-        for i in range(max(low, 0), high):
-            stages[k][1](i)
-
-    left_over = [nz - lag for lag, _stage in stages]
-    add_core(nz - 1)
-    catch_up(1, left_over[1], nz - 1)
-    catch_up(2, left_over[2], nz - 3)
-    catch_up(3, left_over[3], nz - 6)
-    add_x1(nz - 1)
-    catch_up(2, max(left_over[2], nz - 3), nz - 1)
-    catch_up(3, max(left_over[3], nz - 6), nz - 4)
-    add_x2(nz - 1)
-    catch_up(3, max(left_over[3], nz - 4), nz - 1)
-    for i in range(nz - 1):
+    lax.fori_loop(pairs - 1, pairs, step, 0)
+
+    last = pairs - 1
+    both(add_core, last)
+    both(add_x1, last - 1)
+    if last >= 2:
+        both(add_x2, last - 2)
+    both(add_x1, last)
+    both(add_x2, last - 1)
+
+    def drain_item(i, _):
         drain(i)
-    add_y(nz - 1)
-    drain(nz - 1)
+        return 0
+
+    lax.fori_loop(0, nz - 4, drain_item, 0)
+    both(add_x2, last)
+    lax.fori_loop(nz - 4, nz, drain_item, 0)
     total_y = flag[2]
     for n, copy in enumerate(flag_ys):
         copy.wait()
@@ -367,14 +361,17 @@
     for copy in own_copies:
         copy.wait_send()
 
-    for spot in range(owned * lines // pair):
-        column = lax.rem(l * owned + spot * (pair // lines), width)
-        from_x, from_y = column // (width // NX), lax.rem(column, width // NX) // (pair // lines)
-
-        @pl.when(jnp.logical_not(jnp.logical_and(from_x == x, from_y == y)))
-        def _():
-            here = fin.at[pl.ds(spot * pair, pair)]
-            pltpu.make_async_copy(here, here, f_rx.at[spot]).wait()
+    for spot in range(per_owner):
+        from_x = lax.rem(l * owned + spot * UNIT, width) // (width // NX)
+        for i in range(NY):
+            @pl.when(jnp.logical_not(jnp.logical_and(from_x == x, i == y)))
+            def _():
+                here = y_in.at[spot, i]
+                pltpu.make_async_copy(here, here, y_rx.at[spot, i]).wait()
+        total = y_in[spot, 0]
+        for i in range(1, NY):
+            total = total + y_in[spot, i]
+        fin[pl.ds(spot * unit, unit), :] = total
     for n in range(lines):
         out[:, pl.ds(n * 128, 128)] = fin[pl.ds(n, owned, stride=lines), :]
 
@@ -387,7 +384,7 @@
     lines = rows // 128
     owned = nz * width // (2 * NX * NY)
     piece = width // NX * lines
-    pair = piece // NY
+    unit = UNIT * lines
     columns = b_occ.shape[1]
     dma = pltpu.SemaphoreType.DMA
     f32, bf16 = jnp.float32, jnp.bfloat16
@@ -398,15 +395,14 @@
         pltpu.SMEM((columns, blocks), jnp.int32),
         pltpu.VMEM((columns, blocks, 16, BLOCK), bf16),
         pltpu.VMEM((columns, blocks, 16, BLOCK), bf16),
-        pltpu.VMEM((width, depth), bf16),
+        pltpu.VMEM((2 * width, depth), bf16),
         pltpu.VMEM((nz, width, slots * BLOCK), bf16),
         pltpu.VMEM((nz, width * lines, 128), f32),
         pltpu.VMEM((nz, width * lines, 128), f32),
         pltpu.VMEM((nz, 2, piece // 2, 128), f32),
         pltpu.VMEM((nz, 2, piece, 128), f32),
         pltpu.VMEM((nz, piece, 128), f32),
-        pltpu.VMEM((nz, NY - 1, pair, 128), f32),
-        pltpu.VMEM((nz, pair, 128), f32),
+        pltpu.VMEM((owned // UNIT, NY, unit, 128), f32),
         pltpu.VMEM((owned * lines, 128), f32),
         pltpu.VMEM((3, 8, 128), f32),
         pltpu.VMEM((8, 128), f32),
@@ -414,7 +410,7 @@
         pltpu.VMEM((NY - 1, 8, 128), f32),
         dma((4,)), dma((2, 2)), dma((nz, 2)), dma((nz, 2)),
         dma((nz,)), dma((nz,)), dma((nz, 2)), dma((nz, 2)), dma((nz, 2)), dma((nz, 2)),
-        dma((nz, NY - 1)), dma((nz, NY - 1)), dma((nz,)), dma((owned * lines // pair,)),
+        dma((nz, piece // unit)), dma((owned // UNIT, NY)),
         dma(()), dma(()), dma((NX - 1,)), dma((NX - 1,)), dma((NY - 1,)), dma((NY - 1,)),
     ]
     anywhere = pl.BlockSpec(memory_space=pl.ANY)

time: 70 us -> 73 us (1.043)
  the two profiles are of different devices: /device:TPU:264 before, /device:TPU:1 now
where the time goes in v3:
time: 73 us; the launch traced here: 72.4 us
  Pallas kernels  68.9 us (94%)
  local copies, waits for them, and re-layouts  2.66 us (4%)
    pallas_call x1, Pallas kernels, sparse_product(): pl.pallas_call(functools.partial(kernel, nz, slots), out_shape=(jax.Shape...  68.9 us
    unnamed x7, local copies, waits for them, and re-layouts  1.47 us

profile of v3, /device:TPU:1, one launch (start us, length us, event | category | flops | bytes accessed | tf_op | source)
XLA Modules:
  0.0 72.4 jit_solution(6972820114755483609)
XLA Ops:
  0.0 0.0 copy-start.3
  0.0 0.0 copy-start.1
  0.0 68.9 %shard_map.48 = (f32[12,1024]{1,0:T(8,128)}, f32[8,128]{1,0:T(8,128)}) custom-call(bf16[1024,2048]{1,0:T(8,128)(2,1)} %a_hbm.1, bf16[64,2048]{1,0:T(8,128)(2,1)} %bitcast.27, s32[8,16]{1,0:T(8,128)} %aocc_hbm.1, s32[6,16]{1,0:T(8,128)} %bitcast.30), custom_call_target="tpu_custom_call" | custom-call | flops 1610612736 | bytes 4194304 | tf_op jit(solution)/shard_map/pallas_call | solution.py:418
  68.9 0.8 %copy.31 = f32[12,1024]{1,0:T(8,128)S(1)} copy(f32[12,1024]{1,0:T(8,128)} %get-tuple-element.103) | data formatting | bytes 98304
  69.7 1.2 %slice.3 = f32[1,1]{1,0:T(1,128)} slice(f32[8,128]{1,0:T(8,128)} %get-tuple-element.102), slice={[0:1], [0:1]} | slice | bytes 8 | tf_op jit(solution)/shard_map/slice | solution.py:462
  71.6 0.0 copy-done.3
  71.6 0.0 copy-done.1
  71.6 0.2 conditional.1
  71.8 0.0 copy-start.2
  71.8 0.6 copy-done.2
Async XLA Ops:
  0.0 71.6 %copy-start.3 = (s32[8,16]{1,0:T(8,128)S(1)}, s32[8,16]{1,0:T(8,128)}, u32[]{:S(2)}) copy-start(s32[8,16]{1,0:T(8,128)} %aocc_hbm.1) | copy-start | bytes 1540
  0.0 71.6 %copy-start.1 = (bf16[2048,64]{0,1:T(8,128)(2,1)S(1)}, bf16[2048,64]{0,1:T(8,128)(2,1)}, u32[]{:S(2)}) copy-start(bf16[2048,64]{0,1:T(8,128)(2,1)} %param.9) | copy-start | bytes 786436
  71.8 0.6 copy-start.2

commit v4 on v2

--- a/solution.py
+++ b/solution.py
@@ -363,7 +363,7 @@
     for n, copy in enumerate(flag_ys):
         copy.wait()
         total_y = total_y + flag_y[n]
-    flag_out[...] = total_y
+    flag_out[0, 0] = jnp.where(jnp.max(total_y) > 0, jnp.int32(1), jnp.int32(0))
     for copy in own_copies:
         copy.wait_send()
 
@@ -421,9 +421,9 @@
     inside = pl.BlockSpec(memory_space=pltpu.VMEM)
     return pl.pallas_call(
         functools.partial(kernel, nz, slots),
-        out_shape=(jax.ShapeDtypeStruct((owned, rows), f32), jax.ShapeDtypeStruct((8, 128), f32)),
+        out_shape=(jax.ShapeDtypeStruct((owned, rows), f32), jax.ShapeDtypeStruct((1, 1), jnp.int32)),
         in_specs=[anywhere] * 4,
-        out_specs=(inside, inside),
+        out_specs=(inside, pl.BlockSpec(memory_space=pltpu.SMEM)),
         scratch_shapes=scratch,
         compiler_params=pltpu.CompilerParams(
             collective_id=0, has_side_effects=True, vmem_limit_bytes=60 * 1024 * 1024

time: 70 us -> 68.6 us (0.980)
  the two profiles are of different devices: /device:TPU:264 before, /device:TPU:1 now
where the time goes in v4:
time: 68.6 us; the launch traced here: 67.2 us
  Pallas kernels  65.1 us (95%)
  local copies, waits for them, and re-layouts  1.48 us (2%)
    pallas_call x1, Pallas kernels, sparse_product(): pl.pallas_call(functools.partial(kernel, nz, slots), out_shape=(jax.Shape...  65.1 us
    unnamed x7, local copies, waits for them, and re-layouts  1.48 us

profile of v4, /device:TPU:1, one launch (start us, length us, event | category | flops | bytes accessed | tf_op | source)
XLA Modules:
  0.0 67.2 jit_solution(2992052976485660587)
XLA Ops:
  0.0 0.0 copy-start.3
  0.0 0.0 copy-start.1
  0.0 65.1 %shard_map.48 = (f32[12,1024]{1,0:T(8,128)}, s32[1,1]{1,0:T(1,128)}) custom-call(bf16[1024,2048]{1,0:T(8,128)(2,1)} %a_hbm.1, bf16[64,2048]{1,0:T(8,128)(2,1)} %bitcast.27, s32[8,16]{1,0:T(8,128)} %aocc_hbm.1, s32[6,16]{1,0:T(8,128)} %bitcast.30), custom_call_target="tpu_custom_call" | custom-call | flops 1610612736 | bytes 4194304 | tf_op jit(solution)/shard_map/pallas_call | solution.py:422
  65.8 0.0 copy-done.3
  65.8 0.0 copy-done.1
  65.8 0.8 %copy.31 = f32[12,1024]{1,0:T(8,128)S(1)} copy(f32[12,1024]{1,0:T(8,128)} %get-tuple-element.103) | data formatting | bytes 98304
  66.6 0.0 copy-start.2
  66.6 0.6 copy-done.2
  (1 shorter events, 0.0 us)
Async XLA Ops:
  0.0 65.8 %copy-start.3 = (s32[8,16]{1,0:T(8,128)S(1)}, s32[8,16]{1,0:T(8,128)}, u32[]{:S(2)}) copy-start(s32[8,16]{1,0:T(8,128)} %aocc_hbm.1) | copy-start | bytes 1540
  0.0 65.8 %copy-start.1 = (bf16[2048,64]{0,1:T(8,128)(2,1)S(1)}, bf16[2048,64]{0,1:T(8,128)(2,1)}, u32[]{:S(2)}) copy-start(bf16[2048,64]{0,1:T(8,128)(2,1)} %param.9) | copy-start | bytes 786436
  66.6 0.6 copy-start.2
